TPU v7x, 256 devices: a whole 4x4x8 slice. The times are simulated.
256 devices in a mesh: dp: 4 (over x), expert: 8 (over z), etp: 8 (over y, core).
Axes of the slice: x: 4, y: 4, z: 8, core: 2. Of those that a mesh axis runs over, the one named last changes fastest.
Arguments:
- grad_output: bfloat16 [2048, 6144], P(('dp', 'expert', 'etp')), may hold values from -6 to 6
- comb_weights: bfloat16 [2048, 4], P(('dp', 'expert', 'etp')), may hold values from 0.099609375 to 1
- expert_ids: int32 [2048, 4], P(('dp', 'expert', 'etp')), may hold values from 0 to 7, all different within a row; in each aligned block of 8 rows (0 to 7, 8 to 15, ...) at most 6 rows name the same one
- down_weight: bfloat16 [8, 6144, 6144], P('expert', 'etp', 'dp'), may hold values from -0.078125 to 0.078125
- gate_weight: bfloat16 [8, 6144, 6144], P('expert', 'dp', 'etp'), may hold values from -0.078125 to 0.078125
- up_weight: bfloat16 [8, 6144, 6144], P('expert', 'dp', 'etp'), may hold values from -0.078125 to 0.078125
- gate_saved: bfloat16 [8, 1536, 6144], P('expert', None, 'etp'), may hold values from -6 to 6
- up_saved: bfloat16 [8, 1536, 6144], P('expert', None, 'etp'), may hold values from -6 to 6
Outputs:
- input_grad: bfloat16 [2048, 6144], P(('dp', 'expert', 'etp'))
Inputs may be any that keep to these rules, and one draw needn't show every extreme that they name: `expert_ids`: each token names 4 different experts; no expert is named by more than 6 of the tokens of one device.
All inputs are finite; a program needn't handle non-finite values.
Results may differ from a plain program's by a relative error of at most 0.0049.
Values may be sent and summed in bfloat16 or wider, within the bound.
A program may use at most 128 MiB of HBM per device.

v0:
```python
import jax
import jax.numpy as jnp
from jax import lax
from jax.sharding import PartitionSpec as P


def swiglu_backward(hidden_raw, weight, gate_pre, up_pre):
    gate_value = gate_pre.astype(jnp.float32)
    up_value = up_pre.astype(jnp.float32)
    sigmoid_gate = jax.nn.sigmoid(gate_value)
    scaled = hidden_raw * weight[:, None]
    gate_grad = (
        scaled * up_value * sigmoid_gate * (1.0 + gate_value * (1.0 - sigmoid_gate))
    ).astype(jnp.bfloat16)
    up_grad = (scaled * gate_value * sigmoid_gate).astype(jnp.bfloat16)
    return (gate_grad, up_grad)


def on_device(
    grad_output, comb_weights, expert_ids, down_weight, gate_weight, up_weight, gate_saved, up_saved
):
    group_count = lax.axis_size("dp")
    expert_count = lax.axis_size("expert")
    tensor_count = lax.axis_size("etp")
    tokens_here, model_width = grad_output.shape
    choices_count = expert_ids.shape[1]
    capacity = min(
        tokens_here, tokens_here * choices_count // expert_count + max(2, tokens_here // 6)
    )
    quarter = model_width // group_count
    labels = jnp.arange(expert_count, dtype=jnp.int32)
    matches = (expert_ids[:, :, None] == labels[None, None, :]).astype(jnp.int32)
    expert_hits = jnp.sum(matches, axis=1)
    before = jnp.cumsum(expert_hits, axis=0) - expert_hits
    position = jnp.sum(matches * before[:, None, :], axis=2)
    target = expert_ids * capacity + position
    slot_labels = jnp.arange(expert_count * capacity, dtype=jnp.int32)
    chosen = slot_labels[:, None, None] == target[None, :, :]
    selector = (
        jnp.any(chosen, axis=2).astype(jnp.bfloat16).reshape(expert_count, capacity, tokens_here)
    )
    pieces = grad_output.reshape(tokens_here, group_count, quarter)
    outgoing = jnp.einsum(
        "ect,tqd->eqcd", selector, pieces, preferred_element_type=jnp.float32
    ).astype(jnp.bfloat16)
    weight_slots = jnp.sum(
        jnp.where(chosen, comb_weights.astype(jnp.float32)[None, :, :], 0.0), axis=(1, 2)
    )
    weight_out = jnp.broadcast_to(
        weight_slots.reshape(expert_count, 1, capacity), (expert_count, group_count, capacity)
    ).astype(jnp.bfloat16)
    arrived, arrived_weight = (
        lax.all_to_all(outgoing, "dp", split_axis=1, concat_axis=1, tiled=True),
        lax.all_to_all(weight_out, "dp", split_axis=1, concat_axis=1, tiled=True),
    )
    copied = jnp.broadcast_to(
        arrived[:, None], (expert_count, tensor_count, group_count, capacity, quarter)
    )
    copied = copied.reshape(expert_count * tensor_count, group_count, capacity, quarter)
    copied_weight = jnp.broadcast_to(
        arrived_weight[:, None], (expert_count, tensor_count, group_count, capacity)
    )
    copied_weight = copied_weight.reshape(expert_count * tensor_count, group_count, capacity)
    routed, routed_weight = (
        lax.all_to_all(copied, ("expert", "etp"), split_axis=0, concat_axis=0, tiled=True),
        lax.all_to_all(copied_weight, ("expert", "etp"), split_axis=0, concat_axis=0, tiled=True),
    )
    slot_total = expert_count * tensor_count * group_count * capacity
    routed = routed.reshape(slot_total, quarter)
    slot_weight = routed_weight.reshape(slot_total).astype(jnp.float32)
    down_local = down_weight[0]
    gate_local = gate_saved[0]
    up_local = up_saved[0]
    partial_value = jnp.einsum("sq,fq->sf", routed, down_local, preferred_element_type=jnp.float32)
    hidden_raw = lax.psum(partial_value, "dp")
    gate_grad, up_grad = swiglu_backward(hidden_raw, slot_weight, gate_local, up_local)
    slot_grad = jnp.einsum(
        "sf,qf->sq", gate_grad, gate_weight[0], preferred_element_type=jnp.float32
    )
    slot_grad = slot_grad + jnp.einsum(
        "sf,qf->sq", up_grad, up_weight[0], preferred_element_type=jnp.float32
    )
    outbound = slot_grad.reshape(expert_count * tensor_count, group_count, capacity, quarter)
    inbound = lax.all_to_all(outbound, ("expert", "etp"), split_axis=0, concat_axis=0, tiled=True)
    inbound = jnp.sum(
        inbound.reshape(expert_count, tensor_count, group_count, capacity, quarter), axis=1
    )
    complete = lax.all_to_all(inbound, "dp", split_axis=1, concat_axis=3, tiled=True)
    complete = complete.reshape(expert_count * capacity, model_width)
    picked = jnp.take(complete, target.reshape(-1), axis=0)
    picked = picked.reshape(tokens_here, choices_count, model_width)
    return jnp.sum(picked, axis=1).astype(jnp.bfloat16)


def solution(mesh):
    in_specs = (
        P(("dp", "expert", "etp"), None),
        P(("dp", "expert", "etp"), None),
        P(("dp", "expert", "etp"), None),
        P("expert", "etp", "dp"),
        P("expert", "dp", "etp"),
        P("expert", "dp", "etp"),
        P("expert", None, "etp"),
        P("expert", None, "etp"),
    )
    out_specs = P(("dp", "expert", "etp"), None)
    return jax.shard_map(
        on_device, mesh=mesh, in_specs=in_specs, out_specs=out_specs, check_vma=False
    )
```

profile of v0, /device:TPU:32, one launch (start us, length us, event | category | flops | bytes accessed | tf_op | source)
XLA Modules:
  0.0 574.1 jit_solution(5975261550007912184)
XLA Ops:
  6.5 0.9 convert_reduce_fusion
  7.5 0.9 select_reduce_fusion.2
  8.4 0.7 compare_and_fusion
  9.2 0.1 copy.61
  9.4 1.2 fusion.9
  10.6 14.3 %all_to_all.40 = bf16[8,4,6,1536]{3,0,2,1:T(8,128)(2,1)S(1)} all-to-all(bf16[8,4,6,1536]{3,0,2,1:T(8,128)(2,1)S(1)} %copy.52), channel_id=1, replica_groups=mesh['dp'=4,'expert'=8,'etp'=8] {'dp'}, dimensions={1} | all-to-all | bytes 1179648 | tf_op jit(solution)/shard_map/all_to_all | solution.py:53
  24.9 0.5 copy.53
  25.4 1.4 broadcast_in_dim.26
  26.8 118.2 %all_to_all.41 = bf16[64,4,6,1536]{3,1,2,0:T(4,128)(2,1)S(1)} all-to-all(bf16[64,4,6,1536]{3,1,2,0:T(4,128)(2,1)S(1)} %bitcast.46), channel_id=1, replica_groups=mesh['dp'=4,'expert'=8,'etp'=8] {'expert','etp'}, dimensions={0} | all-to-all | bytes 9437184 | tf_op jit(solution)/shard_map/all_to_all | solution.py:65
  145.0 4.4 copy.54
  149.4 8.5 %reshape.100 = bf16[1536,1536]{1,0:T(8,128)(2,1)} reshape(bf16[64,4,6,1536]{3,2,1,0:T(8,128)(2,1)} %copy.54) | data formatting | bytes 9437184 | tf_op jit(solution)/shard_map/reshape | solution.py:69
  157.9 9.2 %fusion.16 = f32[1536,768]{1,0:T(8,128)} fusion(bf16[1536,1536]{1,0:T(8,128)(2,1)} %reshape.100, bf16[1,768,1536]{2,1,0:T(8,128)(2,1)} %param.11), kind=kOutput, calls=%fused_computation.22 | convolution fusion | flops 3623878656 | bytes 11796480 | tf_op jit(solution)/shard_map/sq,fq->sf/dot_general | solution.py:74
  167.1 0.7 copy-done.2
  167.7 0.1 select_reduce_fusion.1
  167.9 7.6 %all_to_all.42 = bf16[8,4,6]{2,0,1:T(8,128)(2,1)S(1)} all-to-all(bf16[8,4,6]{2,0,1:T(8,128)(2,1)S(1)} %broadcast_in_dim.50), channel_id=1, replica_groups=mesh['dp'=4,'expert'=8,'etp'=8] {'dp'}, dimensions={1} | all-to-all | bytes 768 | tf_op jit(solution)/shard_map/all_to_all | solution.py:54
  175.6 15.6 %all_to_all.43 = bf16[64,4,6]{2,1,0:T(4,128)(2,1)S(1)} all-to-all(bf16[64,4,6]{2,1,0:T(4,128)(2,1)S(1)} %bitcast.49), channel_id=1, replica_groups=mesh['dp'=4,'expert'=8,'etp'=8] {'expert','etp'}, dimensions={0} | all-to-all | bytes 6144 | tf_op jit(solution)/shard_map/all_to_all | solution.py:66
  191.2 0.1 reshape.106
  191.4 78.0 %all-reduce.2.cloned.1.call-done = f32[1536,768]{1,0:T(8,128)} async-done(((f32[1536,768]{1,0:T(8,128)}), f32[1536,768]{1,0:T(8,128)}) %all-reduce.2.cloned.1.call-update) | async-done | bytes 4718608 | tf_op jit(solution)/shard_map/psum | solution.py:75
  269.4 12.6 %fusion.12 = f32[1536,1536]{1,0:T(8,128)} fusion(bf16[1,1536,768]{2,1,0:T(8,128)(2,1)S(1)} %copy-done, f32[1536,768]{1,0:T(8,128)} %all-reduce.2.cloned.1.call-done, bf16[1,1536,768]{2,1,0:T(8,128)(2,1)} %param.15, bf16[1,1536,768]{2,1,0:T(8,128)(2,1)} %param.14, f32[1536]{0:T(1024)S(1)} %reshape.106), kind=kOutput, calls=%fused_computation.19 | convolution fusion | flops 3639214080 | bytes 21239808 | tf_op jit(solution)/shard_map/sf,qf->sq/dot_general | solution.py:77
  281.9 9.5 %convolution_add_fusion = f32[1536,1536]{1,0:T(8,128)} fusion(f32[1536,1536]{1,0:T(8,128)} %fusion.12, f32[1536,768]{1,0:T(8,128)S(1)} %copy-done.3, bf16[1,1536,768]{2,1,0:T(8,128)(2,1)S(1)} %copy-done.5, bf16[1,1536,768]{2,1,0:T(8,128)(2,1)S(1)} %copy-done.4, f32[1536]{0:T(1024)S(1)} %reshape.106), kind=kOutput, calls=%fused_computation.2 | convolution fusion | flops 3635675136 | bytes 28317696 | tf_op jit(solution)/shard_map/sf,qf->sq/dot_general | solution.py:80
  291.4 11.4 %reshape.102 = f32[64,4,6,1536]{3,2,1,0:T(8,128)} reshape(f32[1536,1536]{1,0:T(8,128)} %convolution_add_fusion) | data formatting | bytes 18874368 | tf_op jit(solution)/shard_map/reshape | solution.py:83
  302.8 17.0 %copy.56 = f32[64,4,6,1536]{3,1,2,0:T(4,128)} copy(f32[64,4,6,1536]{3,2,1,0:T(8,128)} %reshape.102) | data formatting | bytes 18874368 | tf_op jit(solution)/shard_map/reshape | solution.py:83
  319.8 218.2 %all_to_all.44 = f32[64,4,6,1536]{3,1,2,0:T(4,128)S(1)} all-to-all(f32[64,4,6,1536]{3,1,2,0:T(4,128)} %copy.56), channel_id=1, replica_groups=mesh['dp'=4,'expert'=8,'etp'=8] {'expert','etp'}, dimensions={0} | all-to-all | bytes 18874368 | tf_op jit(solution)/shard_map/all_to_all | solution.py:84
  537.9 1.5 bitcast_reduce_fusion
  539.4 1.7 copy.58
  541.1 3.5 all-to-all-start.5
  544.9 16.9 %all-to-all-done.5 = f32[8,4,6,1536]{3,0,2,1:T(8,128)S(1)} async-done(((f32[8,4,6,1536]{3,0,2,1:T(8,128)}), f32[8,4,6,1536]{3,0,2,1:T(8,128)S(1)}, u32[]{:S(2)}, u32[]{:S(2)}) %all-to-all-start.5) | async-done | bytes 1179680 | tf_op jit(solution)/shard_map/all_to_all | solution.py:88
  561.8 0.8 copy.59
  562.6 0.4 copy.66
  563.0 1.7 gather_fusion
  564.6 1.4 gather.7
  566.0 1.2 select_reduce_fusion
  (28 shorter events, 0.7 us)
Async XLA Ops:
  6.5 262.8 %copy-start = (bf16[1,1536,768]{2,1,0:T(8,128)(2,1)S(1)}, bf16[1,1536,768]{2,1,0:T(8,128)(2,1)}, u32[]{:S(2)}) copy-start(bf16[1,1536,768]{2,1,0:T(8,128)(2,1)} %param.12) | copy-start | bytes 7077892
  6.5 262.8 %all-reduce.2.cloned.1.call-start = ((), (), s32[]{:S(2)}) async-start(), calls=%async_computation.6 | async-start | bytes 9437184 | tf_op jit(solution)/shard_map/psum | solution.py:75
  167.0 0.7 copy-start.2
  269.3 12.6 %copy-start.3 = (f32[1536,768]{1,0:T(8,128)S(1)}, f32[1536,768]{1,0:T(8,128)}, u32[]{:S(2)}) copy-start(f32[1536,768]{1,0:T(8,128)} %all-reduce.2.cloned.1.call-done) | copy-start | bytes 14155780
  269.3 12.6 %copy-start.4 = (bf16[1,1536,768]{2,1,0:T(8,128)(2,1)S(1)}, bf16[1,1536,768]{2,1,0:T(8,128)(2,1)}, u32[]{:S(2)}) copy-start(bf16[1,1536,768]{2,1,0:T(8,128)(2,1)} %param.14) | copy-start | bytes 7077892
  269.3 12.6 %copy-start.5 = (bf16[1,1536,768]{2,1,0:T(8,128)(2,1)S(1)}, bf16[1,1536,768]{2,1,0:T(8,128)(2,1)}, u32[]{:S(2)}) copy-start(bf16[1,1536,768]{2,1,0:T(8,128)(2,1)} %param.13) | copy-start | bytes 7077892
  541.1 20.7 %all-to-all-start.5 = ((f32[8,4,6,1536]{3,0,2,1:T(8,128)}), f32[8,4,6,1536]{3,0,2,1:T(8,128)S(1)}, u32[]{:S(2)}, u32[]{:S(2)}) async-start(f32[8,4,6,1536]{3,0,2,1:T(8,128)} %copy.58), calls=%async_computation.5 | async-start | bytes 2359296 | tf_op jit(solution)/shard_map/all_to_all | solution.py:88
  563.0 4.3 copy-start.1
Sparse Core Ops, SparseCore 0:
  167.2 102.1 all-reduce.1
where the time goes:
time: 575 us; the launch traced here: 574 us
  blocking collectives  374 us (65%)
  waiting for transfers between devices  94.9 us (17%)
  local copies, waits for them, and re-layouts  50.4 us (9%)
  matrix products  32.4 us (6%)
  between operations  13.5 us (2%)
    all_to_all x1, blocking collectives, on_device(): lax.all_to_all(outbound, ('expert', 'etp'), split_axis=0, concat_axis=0,...  218 us
    all_to_all x1, blocking collectives, on_device(): lax.all_to_all(copied, ('expert', 'etp'), split_axis=0, concat_axis=0, ti...  118 us
    psum x1, waiting for transfers between devices, on_device(): hidden_raw = lax.psum(partial_value, 'dp')  78 us
    reshape x2, local copies, waits for them, and re-layouts, on_device(): slot_grad.reshape(expert_count * tensor_count, group_count, capacity, qua...  28.4 us
    all_to_all x1, waiting for transfers between devices, on_device(): lax.all_to_all(inbound, 'dp', split_axis=1, concat_axis=3, tiled=True)  16.9 us
    all_to_all x1, blocking collectives, on_device(): lax.all_to_all(copied_weight, ('expert', 'etp'), split_axis=0, concat_axi...  15.6 us
    all_to_all x1, blocking collectives, on_device(): lax.all_to_all(outgoing, 'dp', split_axis=1, concat_axis=1, tiled=True)  14.3 us
    dot_general x1, matrix products, on_device(): jnp.einsum('sf,qf->sq', gate_grad, gate_weight[0], preferred_element_type...  12.6 us
  transfers between devices with their start and end apart: 2, of which 2 were waited for; matrix products, arithmetic and copies ran while one was open for 0% of the time, Pallas kernels for 0%

commit v1 on v0

--- a/solution.py
+++ b/solution.py
@@ -72,7 +72,8 @@
     gate_local = gate_saved[0]
     up_local = up_saved[0]
     partial_value = jnp.einsum("sq,fq->sf", routed, down_local, preferred_element_type=jnp.float32)
-    hidden_raw = lax.psum(partial_value, "dp")
+    shards = lax.all_gather(partial_value, "dp", axis=0, tiled=False)
+    hidden_raw = shards.sum(axis=0)
     gate_grad, up_grad = swiglu_backward(hidden_raw, slot_weight, gate_local, up_local)
     slot_grad = jnp.einsum(
         "sf,qf->sq", gate_grad, gate_weight[0], preferred_element_type=jnp.float32

time: 575 us -> 654 us (1.14)
  waiting for transfers between devices: 94.9 us -> 163 us
  other arithmetic: 5.45 us -> 15.8 us
    all_gather x0 -> x1, waiting for transfers between devices: none -> 147 us  [on_device(): shards = lax.all_gather(partial_value, 'dp', axis=0, tiled=False)]
    psum x1 -> x0, waiting for transfers between devices: 78 us -> none  [on_device(): hidden_raw = lax.psum(partial_value, 'dp')]
    reduce_sum x0 -> x1, other arithmetic: none -> 10.4 us  [on_device(): hidden_raw = shards.sum(axis=0)]
where the time goes in v1:
time: 654 us; the launch traced here: 653 us
  blocking collectives  374 us (57%)
  waiting for transfers between devices  163 us (25%)
  local copies, waits for them, and re-layouts  50.5 us (8%)
  matrix products  32.4 us (5%)
  other arithmetic  15.8 us (2%)
  between operations  13.5 us (2%)
    all_to_all x1, blocking collectives, on_device(): lax.all_to_all(outbound, ('expert', 'etp'), split_axis=0, concat_axis=0,...  218 us
    all_gather x1, waiting for transfers between devices, on_device(): shards = lax.all_gather(partial_value, 'dp', axis=0, tiled=False)  147 us
    all_to_all x1, blocking collectives, on_device(): lax.all_to_all(copied, ('expert', 'etp'), split_axis=0, concat_axis=0, ti...  118 us
    reshape x2, local copies, waits for them, and re-layouts, on_device(): slot_grad.reshape(expert_count * tensor_count, group_count, capacity, qua...  28.5 us
    all_to_all x1, waiting for transfers between devices, on_device(): lax.all_to_all(inbound, 'dp', split_axis=1, concat_axis=3, tiled=True)  16.9 us
    all_to_all x1, blocking collectives, on_device(): lax.all_to_all(copied_weight, ('expert', 'etp'), split_axis=0, concat_axi...  15.6 us
    all_to_all x1, blocking collectives, on_device(): lax.all_to_all(outgoing, 'dp', split_axis=1, concat_axis=1, tiled=True)  14.3 us
  transfers between devices with their start and end apart: 2, of which 2 were waited for; matrix products, arithmetic and copies ran while one was open for 0% of the time, Pallas kernels for 0%

profile of v1, /device:TPU:32, one launch (start us, length us, event | category | flops | bytes accessed | tf_op | source)
XLA Modules:
  0.0 653.1 jit_solution(11724085955026843318)
XLA Ops:
  6.5 0.9 convert_reduce_fusion
  7.5 0.9 select_reduce_fusion.2
  8.4 0.7 compare_and_fusion
  9.2 0.1 copy.61
  9.4 1.2 fusion.8
  10.6 14.3 %all_to_all.40 = bf16[8,4,6,1536]{3,0,2,1:T(8,128)(2,1)S(1)} all-to-all(bf16[8,4,6,1536]{3,0,2,1:T(8,128)(2,1)S(1)} %copy.52), channel_id=1, replica_groups=mesh['dp'=4,'expert'=8,'etp'=8] {'dp'}, dimensions={1} | all-to-all | bytes 1179648 | tf_op jit(solution)/shard_map/all_to_all | solution.py:53
  24.9 0.5 copy.53
  25.4 1.4 broadcast_in_dim.26
  26.8 118.2 %all_to_all.41 = bf16[64,4,6,1536]{3,1,2,0:T(4,128)(2,1)S(1)} all-to-all(bf16[64,4,6,1536]{3,1,2,0:T(4,128)(2,1)S(1)} %bitcast.54), channel_id=1, replica_groups=mesh['dp'=4,'expert'=8,'etp'=8] {'expert','etp'}, dimensions={0} | all-to-all | bytes 9437184 | tf_op jit(solution)/shard_map/all_to_all | solution.py:65
  145.0 4.5 copy.54
  149.4 8.4 %reshape.132 = bf16[1536,1536]{1,0:T(8,128)(2,1)} reshape(bf16[64,4,6,1536]{3,2,1,0:T(8,128)(2,1)} %copy.54) | data formatting | bytes 9437184 | tf_op jit(solution)/shard_map/reshape | solution.py:69
  157.8 9.1 %fusion.14 = f32[1536,768]{1,0:T(8,128)} fusion(bf16[1536,1536]{1,0:T(8,128)(2,1)} %reshape.132, bf16[1,768,1536]{2,1,0:T(8,128)(2,1)} %param.11), kind=kOutput, calls=%fused_computation.22 | convolution fusion | flops 3623878656 | bytes 11796480 | tf_op jit(solution)/shard_map/sq,fq->sf/dot_general | solution.py:74
  167.0 0.7 copy-done.3
  167.9 7.6 %all_to_all.42 = bf16[8,4,6]{2,0,1:T(8,128)(2,1)S(1)} all-to-all(bf16[8,4,6]{2,0,1:T(8,128)(2,1)S(1)} %broadcast_in_dim.50), channel_id=1, replica_groups=mesh['dp'=4,'expert'=8,'etp'=8] {'dp'}, dimensions={1} | all-to-all | bytes 768 | tf_op jit(solution)/shard_map/all_to_all | solution.py:54
  175.5 15.6 %all_to_all.43 = bf16[64,4,6]{2,1,0:T(4,128)(2,1)S(1)} all-to-all(bf16[64,4,6]{2,1,0:T(4,128)(2,1)S(1)} %bitcast.57), channel_id=1, replica_groups=mesh['dp'=4,'expert'=8,'etp'=8] {'expert','etp'}, dimensions={0} | all-to-all | bytes 6144 | tf_op jit(solution)/shard_map/all_to_all | solution.py:66
  191.2 0.1 reshape.138
  191.3 146.5 %all-gather.3.cloned.1.call-done = f32[6144,768]{1,0:T(8,128)} async-done(((f32[1536,768]{1,0:T(8,128)}), f32[6144,768]{1,0:T(8,128)}) %all-gather.3.cloned.1.call-update) | async-done | bytes 18874384 | tf_op jit(solution)/shard_map/all_gather | solution.py:75
  337.8 10.4 %reduce_sum.58 = f32[1536,768]{1,0:T(8,128)} reduce(f32[4,1536,768]{2,1,0:T(8,128)} %bitcast.53, f32[]{:T(128)} %constant.26.clone.1), dimensions={0}, to_apply=%region_4.5 | reduce | flops 3538944 | bytes 23592964 | tf_op jit(solution)/shard_map/reduce_sum | solution.py:76
  348.2 12.7 %fusion.11 = f32[1536,1536]{1,0:T(8,128)} fusion(bf16[1,1536,768]{2,1,0:T(8,128)(2,1)S(1)} %copy-done, bf16[1,1536,768]{2,1,0:T(8,128)(2,1)} %param.14, bf16[1,1536,768]{2,1,0:T(8,128)(2,1)} %param.15, f32[1536,768]{1,0:T(8,128)} %reduce_sum.58, f32[1536]{0:T(1024)S(1)} %reshape.138), kind=kOutput, calls=%fused_computation.19 | convolution fusion | flops 3639214080 | bytes 21239808 | tf_op jit(solution)/shard_map/sf,qf->sq/dot_general | solution.py:78
  360.9 9.5 %convolution_add_fusion = f32[1536,1536]{1,0:T(8,128)} fusion(f32[1536,1536]{1,0:T(8,128)} %fusion.11, bf16[1,1536,768]{2,1,0:T(8,128)(2,1)S(1)} %copy-done.5, bf16[1,1536,768]{2,1,0:T(8,128)(2,1)S(1)} %copy-done.4, f32[1536,768]{1,0:T(8,128)S(1)} %copy-done.2, f32[1536]{0:T(1024)S(1)} %reshape.138), kind=kOutput, calls=%fused_computation.2 | convolution fusion | flops 3635675136 | bytes 28317696 | tf_op jit(solution)/shard_map/sf,qf->sq/dot_general | solution.py:81
  370.3 11.4 %reshape.134 = f32[64,4,6,1536]{3,2,1,0:T(8,128)} reshape(f32[1536,1536]{1,0:T(8,128)} %convolution_add_fusion) | data formatting | bytes 18874368 | tf_op jit(solution)/shard_map/reshape | solution.py:84
  381.8 17.0 %copy.56 = f32[64,4,6,1536]{3,1,2,0:T(4,128)} copy(f32[64,4,6,1536]{3,2,1,0:T(8,128)} %reshape.134) | data formatting | bytes 18874368 | tf_op jit(solution)/shard_map/reshape | solution.py:84
  398.8 218.2 %all_to_all.44 = f32[64,4,6,1536]{3,1,2,0:T(4,128)S(1)} all-to-all(f32[64,4,6,1536]{3,1,2,0:T(4,128)} %copy.56), channel_id=1, replica_groups=mesh['dp'=4,'expert'=8,'etp'=8] {'expert','etp'}, dimensions={0} | all-to-all | bytes 18874368 | tf_op jit(solution)/shard_map/all_to_all | solution.py:85
  617.0 1.5 bitcast_reduce_fusion
  618.5 1.7 copy.58
  620.2 3.5 all-to-all-start.5
  624.0 16.9 %all-to-all-done.5 = f32[8,4,6,1536]{3,0,2,1:T(8,128)S(1)} async-done(((f32[8,4,6,1536]{3,0,2,1:T(8,128)}), f32[8,4,6,1536]{3,0,2,1:T(8,128)S(1)}, u32[]{:S(2)}, u32[]{:S(2)}) %all-to-all-start.5) | async-done | bytes 1179680 | tf_op jit(solution)/shard_map/all_to_all | solution.py:89
  640.9 0.8 copy.59
  641.6 0.4 copy.66
  642.0 1.7 gather_fusion
  643.7 1.4 gather.7
  645.1 1.2 select_reduce_fusion
  (29 shorter events, 0.8 us)
Async XLA Ops:
  6.5 341.7 %copy-start = (bf16[1,1536,768]{2,1,0:T(8,128)(2,1)S(1)}, bf16[1,1536,768]{2,1,0:T(8,128)(2,1)}, u32[]{:S(2)}) copy-start(bf16[1,1536,768]{2,1,0:T(8,128)(2,1)} %param.12) | copy-start | bytes 7077892
  6.5 331.3 %all-gather.3.cloned.1.call-start = ((), (), s32[]{:S(2)}) async-start(), calls=%async_computation.6 | async-start | bytes 23592960 | tf_op jit(solution)/shard_map/all_gather | solution.py:75
  167.0 0.7 copy-start.3
  348.2 12.7 %copy-start.2 = (f32[1536,768]{1,0:T(8,128)S(1)}, f32[1536,768]{1,0:T(8,128)}, u32[]{:S(2)}) copy-start(f32[1536,768]{1,0:T(8,128)} %reduce_sum.58) | copy-start | bytes 14155780
  348.2 12.7 %copy-start.4 = (bf16[1,1536,768]{2,1,0:T(8,128)(2,1)S(1)}, bf16[1,1536,768]{2,1,0:T(8,128)(2,1)}, u32[]{:S(2)}) copy-start(bf16[1,1536,768]{2,1,0:T(8,128)(2,1)} %param.14) | copy-start | bytes 7077892
  348.2 12.7 %copy-start.5 = (bf16[1,1536,768]{2,1,0:T(8,128)(2,1)S(1)}, bf16[1,1536,768]{2,1,0:T(8,128)(2,1)}, u32[]{:S(2)}) copy-start(bf16[1,1536,768]{2,1,0:T(8,128)(2,1)} %param.13) | copy-start | bytes 7077892
  620.2 20.7 %all-to-all-start.5 = ((f32[8,4,6,1536]{3,0,2,1:T(8,128)}), f32[8,4,6,1536]{3,0,2,1:T(8,128)S(1)}, u32[]{:S(2)}, u32[]{:S(2)}) async-start(f32[8,4,6,1536]{3,0,2,1:T(8,128)} %copy.58), calls=%async_computation.5 | async-start | bytes 2359296 | tf_op jit(solution)/shard_map/all_to_all | solution.py:89
  642.0 4.3 copy-start.1
Sparse Core Ops, SparseCore 0:
  167.1 170.6 all-gather.2
